TPU v7x, 128 devices: a whole 4x4x4 slice. The times are simulated.
128 devices in a mesh: ctx: 32 (over z, x_lo, y), tp: 4 (over x_hi, core).
Axes of the slice: x: 4 (x_hi: 2, x_lo: 2; x = x_hi * 2 + x_lo), y: 4, z: 4, core: 2. Of those that a mesh axis runs over, the one named last changes fastest.
Arguments:
- q_self: bfloat16 [6144, 2560], P('ctx', 'tp'), may hold values from -64 to 64
- k_self: bfloat16 [6144, 2560], P('ctx', 'tp'), may hold values from -64 to 64
- v_self: bfloat16 [6144, 2560], P('ctx', 'tp'), may hold values from -6 to 6
- grad_self: bfloat16 [6144, 2560], P('ctx', 'tp'), may hold values from -448 to 448
- q_cross: bfloat16 [6144, 2560], P('ctx', 'tp'), may hold values from -64 to 64
- grad_cross: bfloat16 [6144, 2560], P('ctx', 'tp'), may hold values from -80 to 80
- k_text: bfloat16 [512, 2560], P(None, 'tp'), may hold values from -64 to 64
- v_text: bfloat16 [512, 2560], P(None, 'tp'), may hold values from -6 to 6
- gain_q: float32 [2560], P('tp'), may hold values from 0.1 to 1.9
- gain_k: float32 [2560], P('tp'), may hold values from 0.1 to 1.9
- gain_cross_q: float32 [2560], P('tp'), may hold values from 0.1 to 1.9
- gain_text_k: float32 [2560], P('tp'), may hold values from 0.1 to 1.9
Outputs:
- grad_q_self: bfloat16 [6144, 2560], P('ctx', 'tp')
- grad_k_self: bfloat16 [6144, 2560], P('ctx', 'tp')
- grad_v_self: bfloat16 [6144, 2560], P('ctx', 'tp')
- grad_q_cross: bfloat16 [6144, 2560], P('ctx', 'tp')
- grad_k_text: bfloat16 [512, 2560], P(None, 'tp')
- grad_v_text: bfloat16 [512, 2560], P(None, 'tp')
All inputs are finite; a program needn't handle non-finite values.
Results may differ from a plain program's by a relative error of at most 0.034.
Values may be sent and summed in bfloat16 or wider, within the bound.
No kernel may reach another device: no remote copies, remote signals or barrier semaphores. Data moves between devices by JAX's collectives and lax.ppermute only.
A program may use at most 192 MiB of HBM per device.

v0:
```python
import jax
import jax.numpy as jnp
from jax import lax
from jax.sharding import PartitionSpec as P

HD = 128
epsilon = 1e-06


def squares(tensor):
    floats = tensor.astype(jnp.float32)
    return jnp.sum(floats * floats, axis=1)


def normalize(tensor, square_sum, gain, features):
    inverse = lax.rsqrt(square_sum / features + epsilon)[:, None]
    return ((tensor.astype(jnp.float32) * inverse * gain).astype(jnp.bfloat16), inverse)


def by_heads(tensor):
    return tensor.reshape(tensor.shape[0], -1, HD)


def into_blocks(tensor, span):
    return tensor.reshape(tensor.shape[0] // span, span, -1, HD)


def start_state(query_heads):
    row_count = query_heads.shape[0]
    head_count = query_heads.shape[1]
    return (
        jnp.full((head_count, row_count), -1e30, jnp.float32),
        jnp.zeros((head_count, row_count), jnp.float32),
        jnp.zeros((head_count, row_count), jnp.float32),
    )


def forward_step(running, query_heads, grad_heads, key_heads, value_heads):
    maximum, totals, weighted = running
    scores = jnp.einsum(
        "qhd,khd->hqk", query_heads, key_heads, preferred_element_type=jnp.float32
    ) * HD ** (-0.5)
    grad_prob = jnp.einsum(
        "qhd,khd->hqk", grad_heads, value_heads, preferred_element_type=jnp.float32
    )
    new_max = jnp.maximum(maximum, jnp.max(scores, axis=2))
    factor = jnp.exp(maximum - new_max)
    weights = jnp.exp(scores - new_max[:, :, None])
    totals = totals * factor + jnp.sum(weights, axis=2)
    weighted = weighted * factor + jnp.sum(weights * grad_prob, axis=2)
    return (new_max, totals, weighted)


def finish(running):
    maximum, totals, weighted = running
    return (maximum + jnp.log(totals), weighted / totals)


def backward_terms(query_heads, grad_heads, logsum, deltas, key_heads, value_heads):
    scaling = HD ** (-0.5)
    scores = (
        jnp.einsum("qhd,khd->hqk", query_heads, key_heads, preferred_element_type=jnp.float32)
        * scaling
    )
    probability = jnp.exp(scores - logsum[:, :, None])
    grad_prob = jnp.einsum(
        "qhd,khd->hqk", grad_heads, value_heads, preferred_element_type=jnp.float32
    )
    grad_score = (probability * (grad_prob - deltas[:, :, None])).astype(jnp.bfloat16)
    results = []
    results.append(
        jnp.einsum("hqk,khd->qhd", grad_score, key_heads, preferred_element_type=jnp.float32)
        * scaling
    )
    results.append(
        jnp.einsum("hqk,qhd->khd", grad_score, query_heads, preferred_element_type=jnp.float32)
        * scaling
    )
    results.append(
        jnp.einsum(
            "hqk,qhd->khd",
            probability.astype(jnp.bfloat16),
            grad_heads,
            preferred_element_type=jnp.float32,
        )
    )
    return results


def forward_pass(query_heads, grad_heads, key_blocks, value_blocks):

    def forward_advance(running, blocks):
        return (forward_step(running, query_heads, grad_heads, blocks[0], blocks[1]), None)

    return lax.scan(forward_advance, start_state(query_heads), (key_blocks, value_blocks))[0]


def query_pass(query_heads, grad_heads, logsum, deltas, key_blocks, value_blocks):

    def query_advance(grad_query, blocks):
        terms = backward_terms(query_heads, grad_heads, logsum, deltas, blocks[0], blocks[1])
        return (grad_query + terms[0], tuple(terms[1:]))

    return lax.scan(
        query_advance, jnp.zeros(query_heads.shape, jnp.float32), (key_blocks, value_blocks)
    )


def norm_terms(tensor, inverse, gain, gradient):
    unit_rows = tensor.astype(jnp.float32) * inverse
    scaled = gradient * gain
    return (unit_rows, scaled, jnp.sum(scaled * unit_rows, axis=1))


def norm_result(inverse, terms, summed, features):
    return (inverse * (terms[1] - terms[0] * (summed / features)[:, None])).astype(jnp.bfloat16)


def local(
    q_self,
    k_self,
    v_self,
    grad_self,
    q_cross,
    grad_cross,
    k_text,
    v_text,
    gain_q,
    gain_k,
    gain_cross_q,
    gain_text_k,
):
    features = q_self.shape[1] * lax.axis_size("tp")
    row_count = q_self.shape[0]
    text_rows = k_text.shape[0]
    span = 4 * row_count
    sums = lax.psum((squares(q_self), squares(k_self), squares(q_cross), squares(k_text)), "tp")
    query_norm, inverse_q = normalize(q_self, sums[0], gain_q, features)
    key_norm, inverse_k = normalize(k_self, sums[1], gain_k, features)
    cross_norm, inverse_c = normalize(q_cross, sums[2], gain_cross_q, features)
    text_norm, inverse_t = normalize(k_text, sums[3], gain_text_k, features)
    query_heads = by_heads(query_norm)
    grad_heads = by_heads(grad_self)
    key_all, value_all = (
        lax.all_gather(key_norm, "ctx", axis=0, tiled=True),
        lax.all_gather(v_self, "ctx", axis=0, tiled=True),
    )
    key_blocks = into_blocks(key_all, span)
    value_blocks = into_blocks(value_all, span)
    logsum, deltas = finish(forward_pass(query_heads, grad_heads, key_blocks, value_blocks))
    grad_query, stacked = query_pass(
        query_heads, grad_heads, logsum, deltas, key_blocks, value_blocks
    )
    grad_key, grad_value = (
        lax.psum_scatter(
            stacked[0].reshape(key_all.shape).astype(jnp.bfloat16),
            "ctx",
            scatter_dimension=0,
            tiled=True,
        ).astype(jnp.float32),
        lax.psum_scatter(
            stacked[1].reshape(key_all.shape).astype(jnp.bfloat16),
            "ctx",
            scatter_dimension=0,
            tiled=True,
        ).astype(jnp.float32),
    )
    cross_heads = by_heads(cross_norm)
    cross_grads = by_heads(grad_cross)
    text_heads = by_heads(text_norm)
    text_values = by_heads(v_text)
    cross_state = forward_step(
        start_state(cross_heads), cross_heads, cross_grads, text_heads, text_values
    )
    cross_logsum, cross_deltas = finish(cross_state)
    cross_terms = backward_terms(
        cross_heads, cross_grads, cross_logsum, cross_deltas, text_heads, text_values
    )
    text_key_grad, text_value_grad = (
        lax.psum(cross_terms[1].reshape(text_rows, -1).astype(jnp.bfloat16), "ctx").astype(
            jnp.float32
        ),
        lax.psum(cross_terms[2].reshape(text_rows, -1).astype(jnp.bfloat16), "ctx").astype(
            jnp.float32
        ),
    )
    pieces_q = norm_terms(q_self, inverse_q, gain_q, grad_query.reshape(row_count, -1))
    pieces_k = norm_terms(k_self, inverse_k, gain_k, grad_key.reshape(row_count, -1))
    pieces_c = norm_terms(q_cross, inverse_c, gain_cross_q, cross_terms[0].reshape(row_count, -1))
    pieces_t = norm_terms(k_text, inverse_t, gain_text_k, text_key_grad)
    row_sums = lax.psum((pieces_q[2], pieces_k[2], pieces_c[2], pieces_t[2]), "tp")
    return (
        norm_result(inverse_q, pieces_q, row_sums[0], features),
        norm_result(inverse_k, pieces_k, row_sums[1], features),
        grad_value.reshape(row_count, -1).astype(jnp.bfloat16),
        norm_result(inverse_c, pieces_c, row_sums[2], features),
        norm_result(inverse_t, pieces_t, row_sums[3], features),
        text_value_grad.astype(jnp.bfloat16),
    )


def solution(mesh):
    in_specs = (
        P("ctx", "tp"),
        P("ctx", "tp"),
        P("ctx", "tp"),
        P("ctx", "tp"),
        P("ctx", "tp"),
        P("ctx", "tp"),
        P(None, "tp"),
        P(None, "tp"),
        P("tp"),
        P("tp"),
        P("tp"),
        P("tp"),
    )
    out_specs = (
        P("ctx", "tp"),
        P("ctx", "tp"),
        P("ctx", "tp"),
        P("ctx", "tp"),
        P(None, "tp"),
        P(None, "tp"),
    )
    return jax.shard_map(local, mesh=mesh, in_specs=in_specs, out_specs=out_specs, check_vma=False)
```

profile of v0, /device:TPU:4, one launch (start us, length us, event | category | flops | bytes accessed | tf_op | source)
XLA Modules:
  0.0 1038.5 jit_solution(16445170293063702059)
XLA Ops:
  12.7 7.4 all-reduce.1
  24.9 2.1 fusion.29
  28.4 2.2 copy.95
  30.6 2.0 multiply_convert_fusion.1
  35.8 154.5 %all-gather.3.cloned.1.call-done = bf16[6144,640]{1,0:T(8,128)(2,1)} async-done(((bf16[192,640]{1,0:T(8,128)(2,1)}), bf16[6144,640]{1,0:T(8,128)(2,1)}) %all-gather.3.cloned.1.call-update) | async-done | bytes 7864336 | tf_op jit(solution)/shard_map/all_gather | solution.py:145
  190.3 18.1 %reshape.100 = bf16[8,768,5,128]{3,2,1,0:T(8,128)(2,1)} reshape(bf16[6144,640]{1,0:T(8,128)(2,1)} %all-gather.3.cloned.1.call-done) | data formatting | bytes 15728640 | tf_op jit(solution)/shard_map/reshape | solution.py:25
  208.4 9.9 copy.75
  218.4 140.3 %all-gather.5.cloned.1.call-done = bf16[6144,640]{1,0:T(8,128)(2,1)} async-done(((bf16[192,640]{1,0:T(8,128)(2,1)}), bf16[6144,640]{1,0:T(8,128)(2,1)}) %all-gather.5.cloned.1.call-update) | async-done | bytes 7864336 | tf_op jit(solution)/shard_map/all_gather | solution.py:146
  358.6 18.1 %reshape.101 = bf16[8,768,5,128]{3,2,1,0:T(8,128)(2,1)} reshape(bf16[6144,640]{1,0:T(8,128)(2,1)} %all-gather.5.cloned.1.call-done) | data formatting | bytes 15728640 | tf_op jit(solution)/shard_map/reshape | solution.py:25
  376.7 10.0 copy.73
  386.7 38.2 %while.30 = (s32[]{:T(128)}, f32[5,192]{1,0:T(8,128)S(1)}, f32[5,192]{1,0:T(8,128)S(1)}, f32[5,192]{1,0:T(8,128)S(1)}, bf16[8,768,5,128]{3,1,2,0:T(8,128)(2,1)},...) while((s32[]{:T(128)}, f32[5,192]{1,0:T(8,128)S(1)}, ...), condition=%wide.region_8.9_spmd.clone, body=%wide.region_4.8_spmd.clone.sunk | while | flops 384129600 | bytes 11374208 | solution.py:95
  386.7 1.8 bitcast_reduce_fusion.2
  388.6 2.1 fusion.112
  391.5 1.8 bitcast_reduce_fusion.2
  393.4 2.1 fusion.112
  396.3 1.8 bitcast_reduce_fusion.2
  398.2 2.1 fusion.112
  401.1 1.8 bitcast_reduce_fusion.2
  402.9 2.1 fusion.112
  405.9 1.8 bitcast_reduce_fusion.2
  407.7 2.1 fusion.112
  410.6 1.8 bitcast_reduce_fusion.2
  412.5 2.1 fusion.112
  415.4 1.8 bitcast_reduce_fusion.2
  417.3 2.1 fusion.112
  420.2 1.8 bitcast_reduce_fusion.2
  422.0 2.1 fusion.112
  425.0 96.3 %while.31 = (s32[]{:T(128)}, f32[192,5,128]{2,0,1:T(8,128)}, bf16[8,768,5,128]{3,1,2,0:T(8,128)(2,1)}, bf16[8,768,5,128]{3,1,2,0:T(8,128)(2,1)}, bf16[8,768,5,12...) while((s32[]{:T(128)}, f32[192,5,128]{2,0,1:T(8,128)}, ...), condition=%wide.region_10.0_spmd.clone, body=%wide.region_9.0_spmd.clone.sunk | while | flops 950476800 | bytes 28028344 | solution.py:104
  426.7 3.2 multiply_convert_fusion.3
  429.9 3.1 fusion.126
  434.8 2.1 bitcast_dynamic-update-slice_fusion.5
  438.7 3.2 multiply_convert_fusion.3
  441.8 3.2 fusion.126
  445.0 1.9 bitcast_dynamic-update-slice_fusion.4
  446.9 2.1 bitcast_dynamic-update-slice_fusion.5
  450.8 3.2 multiply_convert_fusion.3
  453.9 3.2 fusion.126
  459.0 2.1 bitcast_dynamic-update-slice_fusion.5
  462.8 3.2 multiply_convert_fusion.3
  466.0 3.2 fusion.126
  471.0 2.1 bitcast_dynamic-update-slice_fusion.5
  474.8 3.2 multiply_convert_fusion.3
  478.0 3.2 fusion.126
  481.2 1.8 bitcast_dynamic-update-slice_fusion.4
  483.0 2.1 bitcast_dynamic-update-slice_fusion.5
  486.9 3.2 multiply_convert_fusion.3
  490.0 3.2 fusion.126
  493.3 1.8 bitcast_dynamic-update-slice_fusion.4
  495.1 2.1 bitcast_dynamic-update-slice_fusion.5
  499.0 3.2 multiply_convert_fusion.3
  502.1 3.2 fusion.126
  505.3 1.8 bitcast_dynamic-update-slice_fusion.4
  507.1 2.1 bitcast_dynamic-update-slice_fusion.5
  511.0 3.2 multiply_convert_fusion.3
  514.1 3.2 fusion.126
  519.1 2.1 bitcast_dynamic-update-slice_fusion.5
  521.3 11.9 %copy.115 = bf16[8,768,5,128]{3,2,1,0:T(8,128)(2,1)} copy(bf16[8,768,5,128]{3,1,2,0:T(8,128)(2,1)} %get-tuple-element.108) | data formatting | bytes 15728640
  533.2 9.6 copy.124
  542.9 12.0 %copy.116 = bf16[8,768,5,128]{3,2,1,0:T(8,128)(2,1)} copy(bf16[8,768,5,128]{3,1,2,0:T(8,128)(2,1)} %get-tuple-element.109) | data formatting | bytes 15728640
  554.9 9.8 copy.123
  568.8 104.0 %all-reduce.5.cloned.1.call-done = (bf16[512,640]{0,1:T(8,128)(2,1)}, bf16[512,640]{1,0:T(8,128)(2,1)}) async-done(((bf16[512,640]{0,1:T(8,128)(2,1)}, bf16[512,640]{1,0:T(8,128)(2,1)}), (bf16[512,640]{0,1:T(8,128)(2,1)}, bf16[512,640]{1,0:T(8,128)(2,1)})) %all-reduce.5.cloned.1.call-update) | async-done | bytes 1310736 | tf_op jit(solution)/shard_map/psum | solution.py:180
  674.6 179.2 %reduce-scatter.7.cloned.1.call-done = bf16[192,640]{1,0:T(8,128)(2,1)} async-done(((bf16[6144,640]{1,0:T(8,128)(2,1)}), bf16[192,640]{1,0:T(8,128)(2,1)}) %reduce-scatter.7.cloned.1.call-update) | async-done | bytes 245776 | tf_op jit(solution)/shard_map/reduce_scatter | solution.py:155
  854.9 7.3 all-reduce
  867.7 163.5 %reduce-scatter.9.cloned.1.call-done = bf16[192,640]{1,0:T(8,128)(2,1)} async-done(((bf16[6144,640]{1,0:T(8,128)(2,1)}), bf16[192,640]{1,0:T(8,128)(2,1)}) %reduce-scatter.9.cloned.1.call-update) | async-done | bytes 245776
  (166 shorter events, 55.3 us)
Async XLA Ops:
  7.2 12.9 %copy-start.12 = (bf16[192,640]{1,0:T(8,128)(2,1)S(1)}, bf16[192,640]{1,0:T(8,128)(2,1)}, u32[]{:S(2)}) copy-start(bf16[192,640]{1,0:T(8,128)(2,1)} %param.17) | copy-start | bytes 737284
  7.2 12.9 %copy-start.23 = (f32[640]{0:T(1024)S(1)}, f32[640]{0:T(1024)}, u32[]{:S(2)}) copy-start(f32[640]{0:T(1024)} %param.25) | copy-start | bytes 7684
  7.2 14.6 %copy-start.18 = (bf16[192,640]{1,0:T(8,128)(2,1)S(1)}, bf16[192,640]{1,0:T(8,128)(2,1)}, u32[]{:S(2)}) copy-start(bf16[192,640]{1,0:T(8,128)(2,1)} %param.21) | copy-start | bytes 737284
  7.2 14.7 %copy-start.16 = (bf16[512,640]{1,0:T(8,128)(2,1)S(1)}, bf16[512,640]{1,0:T(8,128)(2,1)}, u32[]{:S(2)}) copy-start(bf16[512,640]{1,0:T(8,128)(2,1)} %param.23) | copy-start | bytes 1966084
  7.2 183.1 %all-gather.3.cloned.1.call-start = ((), (), s32[]{:S(2)}) async-start(), calls=%async_computation.2 | async-start | bytes 8110080 | tf_op jit(solution)/shard_map/all_gather | solution.py:145
  8.5 26.5 %copy-start.8 = (bf16[192,640]{0,1:T(8,128)(2,1)}, bf16[192,640]{0,1:T(8,128)(2,1)S(1)}, u32[]{:S(2)}) copy-start(bf16[192,640]{0,1:T(8,128)(2,1)S(1)} %copy.67) | copy-start | bytes 737284
  9.7 13.4 %copy-start.21 = (f32[640]{0:T(1024)S(1)}, f32[640]{0:T(1024)}, u32[]{:S(2)}) copy-start(f32[640]{0:T(1024)} %param.26) | copy-start | bytes 7684
  10.8 12.4 %copy-start.6 = (bf16[192,640]{0,1:T(8,128)(2,1)}, bf16[192,640]{0,1:T(8,128)(2,1)S(1)}, u32[]{:S(2)}) copy-start(bf16[192,640]{0,1:T(8,128)(2,1)S(1)} %copy.83) | copy-start | bytes 737284
  10.9 12.4 %copy-start.22 = (f32[640]{0:T(1024)S(1)}, f32[640]{0:T(1024)}, u32[]{:S(2)}) copy-start(f32[640]{0:T(1024)} %param.27) | copy-start | bytes 7684
  12.3 11.1 %copy-start.2 = (bf16[512,640]{0,1:T(8,128)(2,1)}, bf16[512,640]{0,1:T(8,128)(2,1)S(1)}, u32[]{:S(2)}) copy-start(bf16[512,640]{0,1:T(8,128)(2,1)S(1)} %copy.84) | copy-start | bytes 1966084
  20.9 337.7 %all-gather.5.cloned.1.call-start = ((), (), s32[]{:S(2)}) async-start(), calls=%async_computation.3 | async-start | bytes 8110080 | tf_op jit(solution)/shard_map/all_gather | solution.py:146
  21.7 651.1 %all-reduce.5.cloned.1.call-start = ((), (), s32[]{:S(2)}) async-start(), calls=%async_computation.6 | async-start | bytes 2621440 | tf_op jit(solution)/shard_map/psum | solution.py:180
  23.0 1.8 copy-start.14
  23.4 0.8 copy-start.10
  30.6 4.5 copy-start.20
  32.5 1.0 copy-start.4
  33.5 1.9 copy-start.19
  34.7 819.0 %reduce-scatter.7.cloned.1.call-start = ((), (), s32[]{:S(2)}) async-start(), calls=%async_computation.4 | async-start | bytes 8110080 | tf_op jit(solution)/shard_map/reduce_scatter | solution.py:155
  429.9 3.1 copy-start
  441.8 3.2 copy-start
  453.9 3.2 copy-start
  466.0 3.2 copy-start
  478.0 3.2 copy-start
  490.0 3.2 copy-start
  502.1 3.2 copy-start
  514.1 3.2 copy-start
  542.9 488.3 %reduce-scatter.9.cloned.1.call-start = ((), (), s32[]{:S(2)}) async-start(), calls=%async_computation.5 | async-start | bytes 8110080
  564.7 1.2 copy-start.5
  564.7 1.4 copy-start.11
  566.1 2.5 copy-start.7
  566.1 106.7 %copy-start.3 = (bf16[512,640]{0,1:T(8,128)(2,1)S(1)}, bf16[512,640]{0,1:T(8,128)(2,1)}, u32[]{:S(2)}) copy-start(bf16[512,640]{0,1:T(8,128)(2,1)} %copy-done.2) | copy-start | bytes 1966084
  566.1 108.1 %copy-start.1 = (f32[192,5,128]{2,0,1:T(8,128)S(1)}, f32[192,5,128]{2,0,1:T(8,128)}, u32[]{:S(2)}) copy-start(f32[192,5,128]{2,0,1:T(8,128)} %get-tuple-element.107) | copy-start | bytes 1474564
  566.1 108.3 %copy-start.9 = (bf16[192,640]{0,1:T(8,128)(2,1)S(1)}, bf16[192,640]{0,1:T(8,128)(2,1)}, u32[]{:S(2)}) copy-start(bf16[192,640]{0,1:T(8,128)(2,1)} %copy-done.8) | copy-start | bytes 737284
  567.3 286.5 %copy-start.13 = (bf16[192,640]{1,0:T(8,128)(2,1)S(1)}, bf16[192,640]{1,0:T(8,128)(2,1)}, u32[]{:S(2)}) copy-start(bf16[192,640]{1,0:T(8,128)(2,1)} %param.17) | copy-start | bytes 737284
  862.3 4.4 copy-start.15
  863.2 168.0 %copy-start.17 = (bf16[512,640]{1,0:T(8,128)(2,1)S(1)}, bf16[512,640]{1,0:T(8,128)(2,1)}, u32[]{:S(2)}) copy-start(bf16[512,640]{1,0:T(8,128)(2,1)} %get-tuple-element.486) | copy-start | bytes 1966084
Sparse Core Ops, SparseCore 0:
  21.1 169.2 all-gather.2
  192.0 166.6 all-gather.4
  361.7 310.9 all-reduce.4
  675.2 178.5 reduce-scatter.6
  856.6 174.5 reduce-scatter.8
where the time goes:
time: 1040 us
  waiting for transfers between devices  742 us (71%)
  matrix products  134 us (13%)
  local copies, waits for them, and re-layouts  116 us (11%)
  other arithmetic  16.5 us (2%)
  blocking collectives  14.6 us (1%)
  between operations  14.2 us (1%)
    reduce_scatter x1, waiting for transfers between devices, local(): lax.psum_scatter(stacked[0].reshape(key_all.shape).astype(jnp.bfloat16),...  179 us
    unnamed x6, waiting for transfers between devices  164 us
    all_gather x1, waiting for transfers between devices, local(): lax.all_gather(key_norm, 'ctx', axis=0, tiled=True)  155 us
    all_gather x1, waiting for transfers between devices, local(): lax.all_gather(v_self, 'ctx', axis=0, tiled=True)  140 us
    psum x1, waiting for transfers between devices, local(): lax.psum(cross_terms[1].reshape(text_rows, -1).astype(jnp.bfloat16), 'ctx')  104 us
    unnamed x64, local copies, waits for them, and re-layouts  75.8 us
    reshape x2, local copies, waits for them, and re-layouts, into_blocks(): return tensor.reshape(tensor.shape[0] // span, span, -1, HD)  36.2 us
    dot_general x9, matrix products, backward_terms(): jnp.einsum('qhd,khd->hqk', grad_heads, value_heads, preferred_element_typ...  27.4 us
  transfers between devices with their start and end apart: 5, of which 5 were waited for; matrix products, arithmetic and copies ran while one was open for 25% of the time, Pallas kernels for 0%

commit v1 on v0

--- a/solution.py
+++ b/solution.py
@@ -143,7 +143,9 @@
     grad_heads = by_heads(grad_self)
     key_all, value_all = (
         lax.all_gather(key_norm, "ctx", axis=0, tiled=True),
-        lax.all_gather(v_self, "ctx", axis=0, tiled=True),
+        jnp.concatenate(
+            lax.all_to_all(jnp.stack([v_self] * lax.axis_size("ctx")), "ctx", 0, 0), axis=0
+        ),
     )
     key_blocks = into_blocks(key_all, span)
     value_blocks = into_blocks(value_all, span)

time: 1040 us -> 967 us (0.930)
  waiting for transfers between devices: 742 us -> 650 us
    all_to_all x0 -> x1, waiting for transfers between devices: none -> 150 us  [local(): lax.all_to_all(jnp.stack([v_self] * lax.axis_size('ctx')), 'ctx', 0, 0)]
    all_gather x1 -> x0, waiting for transfers between devices: 140 us -> none  [local(): lax.all_gather(v_self, 'ctx', axis=0, tiled=True)]
    all_gather x1, waiting for transfers between devices: 155 us -> 58.2 us  [local(): lax.all_gather(key_norm, 'ctx', axis=0, tiled=True)]
    another operation x0 -> x2, local copies, waits for them, and re-layouts: none -> 22.2 us  [the longest x1 18.1 us: into_blocks(): return tensor.reshape(tensor.shape[0] // span, span, -1, HD)]
    reshape x2 -> x1, local copies, waits for them, and re-layouts: 36.2 us -> 18.1 us  [into_blocks(): return tensor.reshape(tensor.shape[0] // span, span, -1, HD)]
    unnamed x6 -> x5, waiting for transfers between devices: 164 us -> 162 us
  transfers between devices with their start and end apart: 5 -> 5, of which waited for: 5 -> 5; matrix products, arithmetic and copies ran while one was open for 25% -> 27% of each run, Pallas kernels for 0% -> 0%
where the time goes in v1:
time: 967 us; the launch traced here: 963 us
  waiting for transfers between devices  650 us (67%)
  matrix products  135 us (14%)
  local copies, waits for them, and re-layouts  119 us (12%)
  other arithmetic  18.7 us (2%)
  blocking collectives  14.6 us (2%)
  between operations  14.2 us (1%)
  starting transfers between devices  10.6 us (1%)
    reduce_scatter x1, waiting for transfers between devices, local(): lax.psum_scatter(stacked[0].reshape(key_all.shape).astype(jnp.bfloat16),...  177 us
    unnamed x5, waiting for transfers between devices  162 us
    all_to_all x1, waiting for transfers between devices, local(): lax.all_to_all(jnp.stack([v_self] * lax.axis_size('ctx')), 'ctx', 0, 0)  150 us
    psum x1, waiting for transfers between devices, local(): lax.psum(cross_terms[1].reshape(text_rows, -1).astype(jnp.bfloat16), 'ctx')  103 us
    unnamed x64, local copies, waits for them, and re-layouts  75.6 us
    all_gather x1, waiting for transfers between devices, local(): lax.all_gather(key_norm, 'ctx', axis=0, tiled=True)  58.2 us
    dot_general x9, matrix products, backward_terms(): jnp.einsum('qhd,khd->hqk', grad_heads, value_heads, preferred_element_typ...  27.4 us
    dot_general x9, matrix products, backward_terms(): jnp.einsum('hqk,khd->qhd', grad_score, key_heads, preferred_element_type=...  27.2 us
  transfers between devices with their start and end apart: 5, of which 5 were waited for; matrix products, arithmetic and copies ran while one was open for 27% of the time, Pallas kernels for 0%

profile of v1, /device:TPU:4, one launch (start us, length us, event | category | flops | bytes accessed | tf_op | source)
XLA Modules:
  0.0 963.0 jit_solution(15267687027118785272)
XLA Ops:
  12.6 7.4 all-reduce.1
  20.9 4.1 stack.2
  25.1 10.3 %all-to-all-start = ((bf16[32,192,640]{2,1,0:T(8,128)(2,1)}), bf16[32,192,640]{2,1,0:T(8,128)(2,1)}, u32[]{:S(2)}, u32[]{:S(2)}) async-start(bf16[32,192,640]{2,1,0:T(8,128)(2,1)} %stack.2), calls=%async_computation | async-start | bytes 15728640 | tf_op jit(solution)/shard_map/all_to_all | solution.py:147
  38.5 2.1 fusion.29
  42.1 2.2 copy.95
  44.3 2.0 multiply_convert_fusion.1
  49.5 149.5 %all-to-all-done = bf16[32,192,640]{2,1,0:T(8,128)(2,1)} async-done(((bf16[32,192,640]{2,1,0:T(8,128)(2,1)}), bf16[32,192,640]{2,1,0:T(8,128)(2,1)}, u32[]{:S(2)}, u32[]{:S(2)}) %all-to-all-start) | async-done | bytes 7864352 | tf_op jit(solution)/shard_map/all_to_all | solution.py:147
  199.0 18.1 %reshape.99 = bf16[8,768,5,128]{3,2,1,0:T(8,128)(2,1)} reshape(bf16[32,192,640]{2,1,0:T(8,128)(2,1)} %all-to-all-done) | data formatting | bytes 15728640 | tf_op jit(solution)/shard_map/reshape;reshape | solution.py:25
  217.1 9.9 %copy.73 = bf16[8,768,5,128]{3,1,2,0:T(8,128)(2,1)} copy(bf16[8,768,5,128]{3,2,1,0:T(8,128)(2,1)} %reshape.99) | data formatting | bytes 15728640
  227.0 58.2 %all-gather.2.cloned.1.call-done = bf16[6144,640]{1,0:T(8,128)(2,1)} async-done(((bf16[192,640]{1,0:T(8,128)(2,1)}), bf16[6144,640]{1,0:T(8,128)(2,1)}) %all-gather.2.cloned.1.call-update) | async-done | bytes 7864336 | tf_op jit(solution)/shard_map/all_gather | solution.py:145
  285.2 18.1 %reshape.98 = bf16[8,768,5,128]{3,2,1,0:T(8,128)(2,1)} reshape(bf16[6144,640]{1,0:T(8,128)(2,1)} %all-gather.2.cloned.1.call-done) | data formatting | bytes 15728640 | tf_op jit(solution)/shard_map/reshape | solution.py:25
  303.3 10.0 %copy.75 = bf16[8,768,5,128]{3,1,2,0:T(8,128)(2,1)} copy(bf16[8,768,5,128]{3,2,1,0:T(8,128)(2,1)} %reshape.98) | data formatting | bytes 15728640
  313.3 38.2 %while.30 = (s32[]{:T(128)}, f32[5,192]{1,0:T(8,128)S(1)}, f32[5,192]{1,0:T(8,128)S(1)}, f32[5,192]{1,0:T(8,128)S(1)}, bf16[8,768,5,128]{3,1,2,0:T(8,128)(2,1)},...) while((s32[]{:T(128)}, f32[5,192]{1,0:T(8,128)S(1)}, ...), condition=%wide.region_8.9_spmd.clone, body=%wide.region_4.8_spmd.clone.sunk | while | flops 384129600 | bytes 11374208 | solution.py:95
  313.3 1.8 bitcast_reduce_fusion.2
  315.2 2.1 fusion.112
  318.1 1.8 bitcast_reduce_fusion.2
  320.0 2.1 fusion.112
  322.9 1.8 bitcast_reduce_fusion.2
  324.8 2.1 fusion.112
  327.7 1.8 bitcast_reduce_fusion.2
  329.5 2.1 fusion.112
  332.5 1.8 bitcast_reduce_fusion.2
  334.3 2.1 fusion.112
  337.2 1.8 bitcast_reduce_fusion.2
  339.1 2.1 fusion.112
  342.0 1.8 bitcast_reduce_fusion.2
  343.9 2.1 fusion.112
  346.8 1.8 bitcast_reduce_fusion.2
  348.7 2.1 fusion.112
  351.6 96.3 %while.31 = (s32[]{:T(128)}, f32[192,5,128]{2,0,1:T(8,128)}, bf16[8,768,5,128]{3,1,2,0:T(8,128)(2,1)}, bf16[8,768,5,128]{3,1,2,0:T(8,128)(2,1)}, bf16[8,768,5,12...) while((s32[]{:T(128)}, f32[192,5,128]{2,0,1:T(8,128)}, ...), condition=%wide.region_10.0_spmd.clone, body=%wide.region_9.0_spmd.clone.sunk | while | flops 950476800 | bytes 28028344 | solution.py:104
  353.3 3.2 multiply_convert_fusion.3
  356.5 3.1 fusion.126
  361.4 2.1 bitcast_dynamic-update-slice_fusion.5
  365.2 3.2 multiply_convert_fusion.3
  368.4 3.2 fusion.126
  371.6 1.9 bitcast_dynamic-update-slice_fusion.4
  373.5 2.1 bitcast_dynamic-update-slice_fusion.5
  377.4 3.2 multiply_convert_fusion.3
  380.5 3.2 fusion.126
  385.5 2.1 bitcast_dynamic-update-slice_fusion.5
  389.4 3.2 multiply_convert_fusion.3
  392.6 3.2 fusion.126
  397.6 2.1 bitcast_dynamic-update-slice_fusion.5
  401.4 3.2 multiply_convert_fusion.3
  404.6 3.2 fusion.126
  409.6 2.1 bitcast_dynamic-update-slice_fusion.5
  413.5 3.2 multiply_convert_fusion.3
  416.6 3.2 fusion.126
  419.8 1.8 bitcast_dynamic-update-slice_fusion.4
  421.7 2.1 bitcast_dynamic-update-slice_fusion.5
  425.5 3.2 multiply_convert_fusion.3
  428.7 3.2 fusion.126
  433.7 2.1 bitcast_dynamic-update-slice_fusion.5
  437.6 3.2 multiply_convert_fusion.3
  440.7 3.2 fusion.126
  445.7 2.1 bitcast_dynamic-update-slice_fusion.5
  447.9 12.0 %copy.115 = bf16[8,768,5,128]{3,2,1,0:T(8,128)(2,1)} copy(bf16[8,768,5,128]{3,1,2,0:T(8,128)(2,1)} %get-tuple-element.108) | data formatting | bytes 15728640
  459.8 9.6 copy.124
  469.5 12.0 %copy.116 = bf16[8,768,5,128]{3,2,1,0:T(8,128)(2,1)} copy(bf16[8,768,5,128]{3,1,2,0:T(8,128)(2,1)} %get-tuple-element.109) | data formatting | bytes 15728640
  481.5 9.8 %copy.123 = bf16[768,8,5,128]{3,1,2,0:T(8,128)(2,1)} copy(bf16[768,8,5,128]{3,2,1,0:T(8,128)(2,1)} %bitcast.137) | data formatting | bytes 15728640
  494.6 103.3 %all-reduce.5.cloned.1.call-done = (bf16[512,640]{0,1:T(8,128)(2,1)}, bf16[512,640]{1,0:T(8,128)(2,1)}) async-done(((bf16[512,640]{0,1:T(8,128)(2,1)}, bf16[512,640]{1,0:T(8,128)(2,1)}), (bf16[512,640]{0,1:T(8,128)(2,1)}, bf16[512,640]{1,0:T(8,128)(2,1)})) %all-reduce.5.cloned.1.call-update) | async-done | bytes 1310736 | tf_op jit(solution)/shard_map/psum | solution.py:182
  601.6 177.1 %reduce-scatter.7.cloned.1.call-done = bf16[192,640]{1,0:T(8,128)(2,1)} async-done(((bf16[6144,640]{1,0:T(8,128)(2,1)}), bf16[192,640]{1,0:T(8,128)(2,1)}) %reduce-scatter.7.cloned.1.call-update) | async-done | bytes 245776 | tf_op jit(solution)/shard_map/reduce_scatter | solution.py:157
  779.8 7.3 all-reduce
  793.7 162.0 %reduce-scatter.9.cloned.1.call-done = bf16[192,640]{1,0:T(8,128)(2,1)} async-done(((bf16[6144,640]{1,0:T(8,128)(2,1)}), bf16[192,640]{1,0:T(8,128)(2,1)}) %reduce-scatter.9.cloned.1.call-update) | async-done | bytes 245776
  (166 shorter events, 60.4 us)
Async XLA Ops:
  7.2 12.9 %copy-start.11 = (bf16[192,640]{1,0:T(8,128)(2,1)S(1)}, bf16[192,640]{1,0:T(8,128)(2,1)}, u32[]{:S(2)}) copy-start(bf16[192,640]{1,0:T(8,128)(2,1)} %param.17) | copy-start | bytes 737284
  7.2 12.8 %copy-start.23 = (f32[640]{0:T(1024)S(1)}, f32[640]{0:T(1024)}, u32[]{:S(2)}) copy-start(f32[640]{0:T(1024)} %param.25) | copy-start | bytes 7684
  7.2 13.7 %copy-start.17 = (bf16[192,640]{1,0:T(8,128)(2,1)S(1)}, bf16[192,640]{1,0:T(8,128)(2,1)}, u32[]{:S(2)}) copy-start(bf16[192,640]{1,0:T(8,128)(2,1)} %param.18) | copy-start | bytes 737284
  7.2 278.0 %all-gather.2.cloned.1.call-start = ((), (), s32[]{:S(2)}) async-start(), calls=%async_computation.3 | async-start | bytes 8110080 | tf_op jit(solution)/shard_map/all_gather | solution.py:145
  8.5 40.2 %copy-start.8 = (bf16[192,640]{0,1:T(8,128)(2,1)}, bf16[192,640]{0,1:T(8,128)(2,1)S(1)}, u32[]{:S(2)}) copy-start(bf16[192,640]{0,1:T(8,128)(2,1)S(1)} %copy.67) | copy-start | bytes 737284
  10.8 25.9 %copy-start.6 = (bf16[192,640]{0,1:T(8,128)(2,1)}, bf16[192,640]{0,1:T(8,128)(2,1)S(1)}, u32[]{:S(2)}) copy-start(bf16[192,640]{0,1:T(8,128)(2,1)S(1)} %copy.83) | copy-start | bytes 737284
  12.3 24.6 %copy-start.2 = (bf16[512,640]{0,1:T(8,128)(2,1)}, bf16[512,640]{0,1:T(8,128)(2,1)S(1)}, u32[]{:S(2)}) copy-start(bf16[512,640]{0,1:T(8,128)(2,1)S(1)} %copy.84) | copy-start | bytes 1966084
  25.0 10.3 %copy-start.18 = (bf16[192,640]{1,0:T(8,128)(2,1)S(1)}, bf16[192,640]{1,0:T(8,128)(2,1)}, u32[]{:S(2)}) copy-start(bf16[192,640]{1,0:T(8,128)(2,1)} %param.21) | copy-start | bytes 737284
  25.0 10.5 %copy-start.15 = (bf16[512,640]{1,0:T(8,128)(2,1)S(1)}, bf16[512,640]{1,0:T(8,128)(2,1)}, u32[]{:S(2)}) copy-start(bf16[512,640]{1,0:T(8,128)(2,1)} %param.23) | copy-start | bytes 1966084
  25.0 11.7 %copy-start.21 = (f32[640]{0:T(1024)S(1)}, f32[640]{0:T(1024)}, u32[]{:S(2)}) copy-start(f32[640]{0:T(1024)} %param.26) | copy-start | bytes 7684
  25.0 11.8 %copy-start.22 = (f32[640]{0:T(1024)S(1)}, f32[640]{0:T(1024)}, u32[]{:S(2)}) copy-start(f32[640]{0:T(1024)} %param.27) | copy-start | bytes 7684
  25.1 174.0 %all-to-all-start = ((bf16[32,192,640]{2,1,0:T(8,128)(2,1)}), bf16[32,192,640]{2,1,0:T(8,128)(2,1)}, u32[]{:S(2)}, u32[]{:S(2)}) async-start(bf16[32,192,640]{2,1,0:T(8,128)(2,1)} %stack.2), calls=%async_computation | async-start | bytes 15728640 | tf_op jit(solution)/shard_map/all_to_all | solution.py:147
  35.3 562.5 %all-reduce.5.cloned.1.call-start = ((), (), s32[]{:S(2)}) async-start(), calls=%async_computation.6 | async-start | bytes 2621440 | tf_op jit(solution)/shard_map/psum | solution.py:182
  36.7 1.8 copy-start.13
  37.1 0.8 copy-start.10
  44.3 4.5 copy-start.20
  46.3 1.0 copy-start.4
  47.2 1.9 copy-start.19
  48.4 730.2 %reduce-scatter.7.cloned.1.call-start = ((), (), s32[]{:S(2)}) async-start(), calls=%async_computation.4 | async-start | bytes 8110080 | tf_op jit(solution)/shard_map/reduce_scatter | solution.py:157
  356.5 3.1 copy-start
  368.4 3.2 copy-start
  380.5 3.2 copy-start
  392.6 3.2 copy-start
  404.6 3.2 copy-start
  416.6 3.2 copy-start
  428.7 3.2 copy-start
  440.7 3.2 copy-start
  469.5 486.1 %reduce-scatter.9.cloned.1.call-start = ((), (), s32[]{:S(2)}) async-start(), calls=%async_computation.5 | async-start | bytes 8110080
  491.3 1.2 copy-start.5
  492.5 1.9 copy-start.7
  492.5 105.4 %copy-start.3 = (bf16[512,640]{0,1:T(8,128)(2,1)S(1)}, bf16[512,640]{0,1:T(8,128)(2,1)}, u32[]{:S(2)}) copy-start(bf16[512,640]{0,1:T(8,128)(2,1)} %copy-done.2) | copy-start | bytes 1966084
  492.5 106.8 %copy-start.1 = (f32[192,5,128]{2,0,1:T(8,128)S(1)}, f32[192,5,128]{2,0,1:T(8,128)}, u32[]{:S(2)}) copy-start(f32[192,5,128]{2,0,1:T(8,128)} %get-tuple-element.107) | copy-start | bytes 1474564
  492.5 107.8 %copy-start.9 = (bf16[192,640]{0,1:T(8,128)(2,1)S(1)}, bf16[192,640]{0,1:T(8,128)(2,1)}, u32[]{:S(2)}) copy-start(bf16[192,640]{0,1:T(8,128)(2,1)} %copy-done.8) | copy-start | bytes 737284
  494.1 284.5 %copy-start.12 = (bf16[192,640]{1,0:T(8,128)(2,1)S(1)}, bf16[192,640]{1,0:T(8,128)(2,1)}, u32[]{:S(2)}) copy-start(bf16[192,640]{1,0:T(8,128)(2,1)} %param.17) | copy-start | bytes 737284
  788.3 4.4 copy-start.14
  789.2 166.4 %copy-start.16 = (bf16[512,640]{1,0:T(8,128)(2,1)S(1)}, bf16[512,640]{1,0:T(8,128)(2,1)}, u32[]{:S(2)}) copy-start(bf16[512,640]{1,0:T(8,128)(2,1)} %get-tuple-element.486) | copy-start | bytes 1966084
Sparse Core Ops, SparseCore 0:
  21.0 264.1 all-gather.1
  288.3 309.4 all-reduce.4
  600.4 178.1 reduce-scatter.6
  781.5 174.0 reduce-scatter.8
